TPU v7x, 32 devices: a whole 2x2x4 slice. The times are simulated.
32 devices in a mesh: seq: 8 (over y, x, core), head: 4 (over z).
Axes of the slice: x: 2, y: 2, z: 4, core: 2. Of those that a mesh axis runs over, the one named last changes fastest.
Arguments:
- inputs: bfloat16 [8192, 5376], P(('seq', 'head')), may hold values from -18 to 18
- queries: bfloat16 [8192, 2048], P('seq', 'head'), may hold values from -12 to 12
- key_rows: bfloat16 [8192, 1024], P('seq', 'head'), may hold values from -12 to 12
- values: bfloat16 [8192, 1024], P('seq', 'head'), may hold values from -6 to 6
- out_grad: bfloat16 [8192, 2048], P('seq', 'head'), may hold values from -6 to 6
- band_start: int32 [8192], P('seq'), may hold values from 0 to 8191, as said below
- owners: int32 [4, 6], replicated, may hold values from 0 to 7, as said below
Outputs:
- left_stat: float32 [8, 4, 1024, 1024], P('seq', 'head')
- right_stat: float32 [8, 4, 1024, 1024], P('seq', 'head')
Inputs may be any that keep to these rules, and one draw needn't show every extreme that they name: band_start[i] lies between i - 1023 and i, and never decreases with i. `owners`: the 6 entries of a row differ.
All inputs are finite; a program needn't handle non-finite values.
Results may differ from a plain program's by a relative error of at most 0.015.
Values may be sent and summed in bfloat16 or wider, within the bound.
A program may use at most 128 MiB of HBM per device.

v0:
```python
import jax
import jax.numpy as jnp
from jax import lax
from jax.sharding import PartitionSpec as P

D = 5376
HD = 128
KV_DEV = 2
QPK = 2
WINDOW = 1024
BLOCK = 1024
NBLK = 6


score_scale = 168.0 ** (-0.5)
rotary_frequency_base = 10000.0
neg_large = -1e30


def shifted(value, axis, steps):
    count = lax.axis_size(axis)
    initial, last = (max(0, -steps), min(count, count - steps))
    return lax.ppermute(value, axis, [(source, source + steps) for source in range(initial, last)])


def rope_tables(positions, head_size):
    half_size = head_size // 2
    frequency = jnp.power(
        rotary_frequency_base, -2.0 * jnp.arange(half_size, dtype=jnp.float32) / head_size
    )
    angles = positions.astype(jnp.float32)[:, None] * frequency[None, :]
    cosine_table = jnp.concatenate([jnp.cos(angles), jnp.cos(angles)], 1)
    sine_table = jnp.concatenate([jnp.sin(angles), jnp.sin(angles)], 1)
    return (cosine_table, sine_table)


def unrotate(gradient, cosine_table, sine_table):
    half_size = gradient.shape[-1] // 2
    scaled = gradient * sine_table
    turned = jnp.concatenate([-scaled[..., half_size:], scaled[..., :half_size]], -1)
    return gradient * cosine_table - turned


def per_device(inputs, queries, key_rows, values, out_grad, band_start, owners):
    tok_rows = queries.shape[0]
    seq_count = lax.axis_size("seq")
    seq_index = lax.axis_index("seq")
    group_index = lax.axis_index("head")
    tokens_all = tok_rows * seq_count
    earlier_keys, earlier_values = shifted((key_rows, values), "seq", 1)
    gathered_key_rows = jnp.concatenate([earlier_keys, key_rows], 0).reshape(
        2 * tok_rows, KV_DEV, HD
    )
    value_all = jnp.concatenate([earlier_values, values], 0).reshape(2 * tok_rows, KV_DEV, HD)
    query_heads = queries.reshape(tok_rows, KV_DEV, QPK, HD)
    out_heads = out_grad.reshape(tok_rows, KV_DEV, QPK, HD)
    block_rows = min(512, tok_rows)
    span_rows = block_rows + WINDOW
    block_count = tok_rows // block_rows

    def one_block(block_index, state_pair):
        grad_query, grad_keys, grad_values = state_pair
        offset = block_index * block_rows
        query_part = lax.dynamic_slice_in_dim(query_heads, offset, block_rows, 0)
        out_part = lax.dynamic_slice_in_dim(out_heads, offset, block_rows, 0)
        key_start = tok_rows + offset - WINDOW
        key_part = lax.dynamic_slice_in_dim(gathered_key_rows, key_start, span_rows, 0)
        value_part = lax.dynamic_slice_in_dim(value_all, key_start, span_rows, 0)
        band_part = lax.dynamic_slice_in_dim(band_start, offset, block_rows, 0)
        query_pos = seq_index * tok_rows + offset + jnp.arange(block_rows, dtype=jnp.int32)
        key_pos = seq_index * tok_rows + offset - WINDOW + jnp.arange(span_rows, dtype=jnp.int32)
        allowed = (key_pos[None, :] >= band_part[:, None]) & (
            key_pos[None, :] <= query_pos[:, None]
        )
        attention_logits = (
            jnp.einsum("qgrh,kgh->grqk", query_part, key_part, preferred_element_type=jnp.float32)
            * score_scale
        )
        masked = jnp.where(allowed, attention_logits, neg_large)
        row_top = jnp.max(masked, -1, keepdims=True)
        exponent = jnp.where(allowed, jnp.exp(masked - row_top), 0.0)
        attend = exponent / jnp.sum(exponent, -1, keepdims=True)
        attend_low = attend.astype(jnp.bfloat16)
        grad_attend = jnp.einsum(
            "qgrh,kgh->grqk", out_part, value_part, preferred_element_type=jnp.float32
        )
        row_dot = jnp.sum(attend * grad_attend, -1, keepdims=True)
        grad_score = (attend * (grad_attend - row_dot) * score_scale).astype(jnp.bfloat16)
        query_term = jnp.einsum(
            "grqk,kgh->qgrh", grad_score, key_part, preferred_element_type=jnp.float32
        )
        key_term = jnp.einsum(
            "grqk,qgrh->kgh", grad_score, query_part, preferred_element_type=jnp.float32
        )
        value_term = jnp.einsum(
            "grqk,qgrh->kgh", attend_low, out_part, preferred_element_type=jnp.float32
        )
        grad_query = lax.dynamic_update_slice_in_dim(grad_query, query_term, offset, 0)
        grad_keys = lax.dynamic_update_slice_in_dim(
            grad_keys,
            lax.dynamic_slice_in_dim(grad_keys, key_start, span_rows, 0) + key_term,
            key_start,
            0,
        )
        grad_values = lax.dynamic_update_slice_in_dim(
            grad_values,
            lax.dynamic_slice_in_dim(grad_values, key_start, span_rows, 0) + value_term,
            key_start,
            0,
        )
        return (grad_query, grad_keys, grad_values)

    start_state = (
        jnp.zeros((tok_rows, KV_DEV, QPK, HD), jnp.float32),
        jnp.zeros((2 * tok_rows, KV_DEV, HD), jnp.float32),
        jnp.zeros((2 * tok_rows, KV_DEV, HD), jnp.float32),
    )
    grad_query, grad_keys, grad_values = lax.fori_loop(0, block_count, one_block, start_state)
    rim_keys, rim_values = (
        shifted(grad_keys[:tok_rows].astype(jnp.bfloat16), "seq", -1).astype(jnp.float32),
        shifted(grad_values[:tok_rows].astype(jnp.bfloat16), "seq", -1).astype(jnp.float32),
    )
    own_keys = grad_keys[tok_rows:] + rim_keys
    own_values = grad_values[tok_rows:] + rim_values
    positions = seq_index * tok_rows + jnp.arange(tok_rows, dtype=jnp.int32)
    cosine_table, sine_table = rope_tables(positions, HD)
    query_pre = unrotate(
        grad_query.reshape(tok_rows, KV_DEV * QPK, HD),
        cosine_table[:, None, :],
        sine_table[:, None, :],
    )
    key_pre = unrotate(own_keys, cosine_table[:, None, :], sine_table[:, None, :])
    column_grads = jnp.concatenate(
        [
            query_pre.reshape(tok_rows, KV_DEV * QPK * HD),
            key_pre.reshape(tok_rows, KV_DEV * HD),
            own_values.reshape(tok_rows, KV_DEV * HD),
        ],
        1,
    ).astype(jnp.bfloat16)
    column_count = column_grads.shape[1]
    partial_sum = lax.dot_general(
        lax.all_gather(inputs, "head", axis=0, tiled=True),
        column_grads,
        (((0,), (0,)), ((), ())),
        preferred_element_type=jnp.float32,
    )
    gradient = lax.psum(partial_sum.astype(jnp.bfloat16), "seq")
    padded = jnp.pad(gradient, ((0, NBLK * BLOCK - D), (0, 0)))
    owner_row = lax.dynamic_index_in_dim(owners, group_index, 0, keepdims=False)
    is_mine = owner_row == seq_index
    block_pick = jnp.sum(jnp.where(is_mine, jnp.arange(NBLK, dtype=jnp.int32), 0))
    block_part = lax.dynamic_slice_in_dim(padded, block_pick * BLOCK, BLOCK, 0)

    def gram_pair(part_rows):
        left_value = (
            lax.dot_general(
                part_rows, part_rows, (((1,), (1,)), ((), ())), preferred_element_type=jnp.float32
            )
            / tokens_all
        )
        right_value = (
            lax.dot_general(
                part_rows, part_rows, (((0,), (0,)), ((), ())), preferred_element_type=jnp.float32
            )
            / tokens_all
        )
        return (left_value, right_value)

    def nothing(part_rows):
        return (
            jnp.zeros((BLOCK, BLOCK), jnp.float32),
            jnp.zeros((column_count, column_count), jnp.float32),
        )

    left_stat, right_stat = lax.cond(jnp.any(is_mine), gram_pair, nothing, block_part)
    return (left_stat[None, None], right_stat[None, None])


def solution(mesh):
    in_specs = (
        P(("seq", "head"), None),
        P("seq", "head"),
        P("seq", "head"),
        P("seq", "head"),
        P("seq", "head"),
        P("seq"),
        P(),
    )
    out_specs = (P("seq", "head", None, None), P("seq", "head", None, None))
    return jax.shard_map(
        per_device, mesh=mesh, in_specs=in_specs, out_specs=out_specs, check_vma=False
    )
```

profile of v0, /device:TPU:0, one launch (start us, length us, event | category | flops | bytes accessed | tf_op | source)
XLA Modules:
  0.0 411.6 jit_solution(8158723403627443930)
XLA Ops:
  9.2 3.1 collective-permute-start
  13.6 3.8 collective-permute-start.1
  18.4 1.3 copy.28
  19.7 2.4 copy.31
  23.8 2.1 pad_maximum_fusion.1
  26.0 1.6 broadcast.83
  27.6 1.6 broadcast.83.clone
  29.2 1.6 broadcast_in_dim.95
  30.7 139.1 %while.22 = (s32[]{:T(128)}, f32[1024,2,2,128]{0,3,2,1:T(8,128)}, f32[2048,2,128]{0,2,1:T(8,128)}, f32[2048,2,128]{0,2,1:T(8,128)}, bf16[2048,2,128]{0,2,1:T(8,1...) while((s32[]{:T(128)}, f32[1024,2,2,128]{0,3,2,1:T(8,128)}, ...), condition=%wide.region_5.6_spmd, body=%wide.region_1.5_spmd.sunk | while | flops 4095748608 | bytes 186194320 | solution.py:118
  31.5 11.7 %fusion.115 = (f32[2,2,512]{2,1,0:T(2,128)S(1)}, f32[2,2,512,1536]{2,3,1,0:T(8,128)}) fusion(pred[512,1536]{0,1:T(8,128)(4,1)S(1)} %compare_and_fusion.2, bf16[2048,2,128]{0,2,1:T(8,128)(2,1)} %get-tuple-element.555, s32[]{:T(128)S(6)} %select_n.101, bf16[1024,2,2,128]{0,3,2,1:T(8,128)(2,1)} %get-tuple-element.558, s32[]{:T(128)S(6)} %select_n.100), kind=kOutput, calls=%fused_computation.99.clone.1 | convolution fusion | flops 821036544 | bytes 15474696 | tf_op jit(solution)/shard_map/while/body/eval_jaxpr/sub | solution.py:81
  43.3 7.6 %fusion.114 = f32[2,1536,512,2]{2,1,3,0:T(8,128)} fusion(bf16[2048,2,128]{0,2,1:T(8,128)(2,1)S(1)} %get-tuple-element.559, s32[]{:T(128)S(6)} %select_n.101, bf16[1024,2,2,128]{0,3,2,1:T(8,128)(2,1)} %get-tuple-element.560, s32[]{:T(128)S(6)} %select_n.100), kind=kOutput, calls=%fused_computation.33.clone.1 | convolution fusion | flops 805306368 | bytes 13893640 | tf_op jit(solution)/shard_map/while/body/eval_jaxpr/qgrh,kgh->grqk/dot_general | solution.py:84
  50.8 20.2 %fusion.117 = f32[2048,2,128]{0,2,1:T(8,128)S(1)} fusion(f32[2048,2,128]{0,2,1:T(8,128)S(1)} %copy-done.4, s32[]{:T(128)S(6)} %select_n.101, f32[2,1536,512,2]{2,1,3,0:T(8,128)} %fusion.114, bf16[1024,2,2,128]{0,3,2,1:T(8,128)(2,1)} %get-tuple-element.558, s32[]{:T(128)S(6)} %select_n.100, f32[2,2,512,1536]{2,3,1,0:T(8,128)} %get-tuple-element.517, ...), kind=kOutput, calls=%fused_computation.25.clone.1 | convolution fusion | flops 827723264 | bytes 54018056 | tf_op jit(solution)/shard_map/while/body/eval_jaxpr/grqk,qgrh->kgh/dot_general | solution.py:92
  71.0 1.3 copy-done.5
  72.3 8.8 %fusion.118 = f32[2048,2,128]{0,2,1:T(8,128)} fusion(f32[2048,2,128]{0,2,1:T(8,128)} %get-tuple-element.538, s32[]{:T(128)S(6)} %select_n.101, bf16[1024,2,2,128]{0,3,2,1:T(8,128)(2,1)} %get-tuple-element.560, s32[]{:T(128)S(6)} %select_n.100, f32[2,2,512,1536]{2,3,1,0:T(8,128)} %get-tuple-element.517, f32[2,2,512]{2,1,0:T(2,128)S(1)} %get-tuple-element.518), kind=kOutput, calls=%fused_computation.22.clone.1 | convolution fusion | flops 811991040 | bytes 16261128 | tf_op jit(solution)/shard_map/while/body/eval_jaxpr/grqk,qgrh->kgh/dot_general | solution.py:95
  81.1 17.9 %fusion.116 = f32[1024,2,2,128]{0,3,2,1:T(8,128)S(1)} fusion(f32[1024,2,2,128]{0,3,2,1:T(8,128)S(1)} %copy-done.1, s32[]{:T(128)S(6)} %select_n.100, f32[2,1536,512,2]{2,1,3,0:T(8,128)} %fusion.114, bf16[2048,2,128]{0,2,1:T(8,128)(2,1)} %get-tuple-element.555, s32[]{:T(128)S(6)} %select_n.101, f32[2,2,512,1536]{2,3,1,0:T(8,128)} %get-tuple-element.517, ...), kind=kOutput, calls=%fused_computation.27.clone.1 | convolution fusion | flops 827330048 | bytes 52183048 | tf_op jit(solution)/shard_map/while/body/eval_jaxpr/grqk,kgh->qgrh/dot_general | solution.py:89
  99.0 1.3 copy-done.2
  101.1 11.7 %fusion.115 = (f32[2,2,512]{2,1,0:T(2,128)S(1)}, f32[2,2,512,1536]{2,3,1,0:T(8,128)}) fusion(pred[512,1536]{0,1:T(8,128)(4,1)S(1)} %compare_and_fusion.2, bf16[2048,2,128]{0,2,1:T(8,128)(2,1)} %get-tuple-element.555, s32[]{:T(128)S(6)} %select_n.101, bf16[1024,2,2,128]{0,3,2,1:T(8,128)(2,1)} %get-tuple-element.558, s32[]{:T(128)S(6)} %select_n.100), kind=kOutput, calls=%fused_computation.99.clone.1 | convolution fusion | flops 821036544 | bytes 15474696 | tf_op jit(solution)/shard_map/while/body/eval_jaxpr/sub | solution.py:81
  112.8 7.6 %fusion.114 = f32[2,1536,512,2]{2,1,3,0:T(8,128)} fusion(bf16[2048,2,128]{0,2,1:T(8,128)(2,1)S(1)} %get-tuple-element.559, s32[]{:T(128)S(6)} %select_n.101, bf16[1024,2,2,128]{0,3,2,1:T(8,128)(2,1)} %get-tuple-element.560, s32[]{:T(128)S(6)} %select_n.100), kind=kOutput, calls=%fused_computation.33.clone.1 | convolution fusion | flops 805306368 | bytes 13893640 | tf_op jit(solution)/shard_map/while/body/eval_jaxpr/qgrh,kgh->grqk/dot_general | solution.py:84
  120.4 20.2 %fusion.117 = f32[2048,2,128]{0,2,1:T(8,128)S(1)} fusion(f32[2048,2,128]{0,2,1:T(8,128)S(1)} %copy-done.4, s32[]{:T(128)S(6)} %select_n.101, f32[2,1536,512,2]{2,1,3,0:T(8,128)} %fusion.114, bf16[1024,2,2,128]{0,3,2,1:T(8,128)(2,1)} %get-tuple-element.558, s32[]{:T(128)S(6)} %select_n.100, f32[2,2,512,1536]{2,3,1,0:T(8,128)} %get-tuple-element.517, ...), kind=kOutput, calls=%fused_computation.25.clone.1 | convolution fusion | flops 827723264 | bytes 54018056 | tf_op jit(solution)/shard_map/while/body/eval_jaxpr/grqk,qgrh->kgh/dot_general | solution.py:92
  140.7 1.3 copy-done.5
  142.0 8.7 %fusion.118 = f32[2048,2,128]{0,2,1:T(8,128)} fusion(f32[2048,2,128]{0,2,1:T(8,128)} %get-tuple-element.538, s32[]{:T(128)S(6)} %select_n.101, bf16[1024,2,2,128]{0,3,2,1:T(8,128)(2,1)} %get-tuple-element.560, s32[]{:T(128)S(6)} %select_n.100, f32[2,2,512,1536]{2,3,1,0:T(8,128)} %get-tuple-element.517, f32[2,2,512]{2,1,0:T(2,128)S(1)} %get-tuple-element.518), kind=kOutput, calls=%fused_computation.22.clone.1 | convolution fusion | flops 811991040 | bytes 16261128 | tf_op jit(solution)/shard_map/while/body/eval_jaxpr/grqk,qgrh->kgh/dot_general | solution.py:95
  150.7 17.8 %fusion.116 = f32[1024,2,2,128]{0,3,2,1:T(8,128)S(1)} fusion(f32[1024,2,2,128]{0,3,2,1:T(8,128)S(1)} %copy-done.1, s32[]{:T(128)S(6)} %select_n.100, f32[2,1536,512,2]{2,1,3,0:T(8,128)} %fusion.114, bf16[2048,2,128]{0,2,1:T(8,128)(2,1)} %get-tuple-element.555, s32[]{:T(128)S(6)} %select_n.101, f32[2,2,512,1536]{2,3,1,0:T(8,128)} %get-tuple-element.517, ...), kind=kOutput, calls=%fused_computation.27.clone.1 | convolution fusion | flops 827330048 | bytes 52183048 | tf_op jit(solution)/shard_map/while/body/eval_jaxpr/grqk,kgh->qgrh/dot_general | solution.py:89
  168.5 1.3 copy-done.2
  175.0 1.9 bitcast_multiply_fusion.16
  180.9 23.9 %all-gather.2.cloned.1.call-done = bf16[1024,5376]{1,0:T(8,128)(2,1)} async-done(((bf16[256,5376]{1,0:T(8,128)(2,1)}), bf16[1024,5376]{1,0:T(8,128)(2,1)}) %all-gather.2.cloned.1.call-update) | async-done | bytes 11010064 | tf_op jit(solution)/shard_map/all_gather | solution.py:143
  204.8 19.3 %fusion.72 = bf16[5376,1024]{0,1:T(8,128)(2,1)} fusion(bf16[1024,5376]{1,0:T(8,128)(2,1)} %all-gather.2.cloned.1.call-done, bf16[1024,256]{0,1:T(8,128)(2,1)S(1)} %bitcast.154, bf16[1024,256]{0,1:T(8,128)(2,1)S(1)} %bitcast.153, bf16[1024,512]{0,1:T(8,128)(2,1)S(1)} %fusion.78), kind=kOutput, calls=%fused_computation.68 | convolution fusion | flops 11286085632 | bytes 24117248 | tf_op jit(solution)/shard_map/dot_general | solution.py:142
  224.1 1.3 fusion.82
  226.1 151.4 %all-reduce.3.cloned.1.call-done = bf16[5376,1024]{0,1:T(8,128)(2,1)} async-done(((bf16[5376,1024]{0,1:T(8,128)(2,1)}), bf16[5376,1024]{0,1:T(8,128)(2,1)}) %all-reduce.3.cloned.1.call-update) | async-done | bytes 11010064 | tf_op jit(solution)/shard_map/psum | solution.py:148
  377.6 27.2 %conditional.1 = (f32[1,1,1024,1024]{3,2,1,0:T(8,128)}, f32[1,1,1024,1024]{3,2,1,0:T(8,128)}) conditional(s32[]{:T(128)} %convert_element_type.55, () %tuple.63, (bf16[5376,1024]{0,1:T(8,128)(2,1)}, pred[1,6]{1,0:T(4,128)(4,1)S(1)}, s32[6]{0:T(128)S(1)}) %tuple.65), branch_computations={%region_7.8_spmd, %region_8.10_spmd} | conditional | flops 4297064448 | bytes 96469120 | solution.py:176
  378.8 14.6 %copy.36 = bf16[5376,1024]{1,0:T(8,128)(2,1)} copy(bf16[5376,1024]{0,1:T(8,128)(2,1)} %get-tuple-element.421) | data formatting | bytes 22020096 | tf_op jit(solution)/shard_map
  393.5 6.8 %multiply_bitcast_fusion = f32[1,1,1024,1024]{3,2,1,0:T(8,128)} fusion(s32[]{:T(128)S(6)} %select_n.79, bf16[5376,1024]{1,0:T(8,128)(2,1)} %copy.36), kind=kOutput, calls=%fused_computation.59 | convolution fusion | flops 2148532224 | bytes 15204356 | tf_op jit(solution)/shard_map/cond/branch_1_fun/dot_general | solution.py:163
  400.3 4.5 %multiply_bitcast_fusion.1 = f32[1,1,1024,1024]{3,2,1,0:T(8,128)} fusion(s32[]{:T(128)S(6)} %select_n.79, bf16[5376,1024]{1,0:T(8,128)(2,1)S(1)} %copy-done), kind=kOutput, calls=%fused_computation.60 | convolution fusion | flops 2148532224 | bytes 15204356 | tf_op jit(solution)/shard_map/cond/branch_1_fun/dot_general | solution.py:157
  (65 shorter events, 17.3 us)
Async XLA Ops:
  7.2 11.2 %copy-start.10 = (bf16[1024,512]{1,0:T(8,128)(2,1)S(1)}, bf16[1024,512]{1,0:T(8,128)(2,1)}, u32[]{:S(2)}) copy-start(bf16[1024,512]{1,0:T(8,128)(2,1)} %param.12) | copy-start | bytes 3145732
  7.2 197.6 %all-gather.2.cloned.1.call-start = ((), (), s32[]{:S(2)}) async-start(), calls=%async_computation | async-start | bytes 13762560 | tf_op jit(solution)/shard_map/all_gather | solution.py:143
  7.9 369.6 %all-reduce.3.cloned.1.call-start = ((), (), s32[]{:S(2)}) async-start(), calls=%async_computation.1 | async-start | bytes 22020096 | tf_op jit(solution)/shard_map/psum | solution.py:148
  9.2 14.6 %collective-permute-start = (bf16[1024,256]{0,1:T(8,128)(2,1)S(1)}, bf16[1024,256]{0,1:T(8,128)(2,1)}, u32[]{:S(2)}, u32[]{:S(2)}) collective-permute-start(bf16[1024,256]{0,1:T(8,128)(2,1)S(1)} %copy.26), channel_id=1, source_target_pairs={{0,4},{4,8},{8,12},{12,16},{16,20},{20,24},{24,28},{1,5},{5,9},{9,... | collective-permute-start | bytes 1572872 | tf_op jit(solution)/shard_map/ppermute | solution.py:23
  13.6 12.3 %collective-permute-start.1 = (bf16[1024,256]{0,1:T(8,128)(2,1)S(1)}, bf16[1024,256]{0,1:T(8,128)(2,1)S(1)}, u32[]{:S(2)}, u32[]{:S(2)}) collective-permute-start(bf16[1024,256]{0,1:T(8,128)(2,1)S(1)} %copy.29), channel_id=1, source_target_pairs={{0,4},{4,8},{8,12},{12,16},{16,20},{20,24},{24,28},{1,5},{5,9},{9,... | collective-permute-start | bytes 1572872 | tf_op jit(solution)/shard_map/ppermute | solution.py:23
  25.9 4.8 %copy-start.11 = (s32[1024]{0:T(1024)S(1)}, s32[1024]{0:T(1024)}, u32[]{:S(2)}) copy-start(s32[1024]{0:T(1024)} %param.16) | copy-start | bytes 12292
  43.3 7.6 %copy-start.4 = (f32[2048,2,128]{0,2,1:T(8,128)S(1)}, f32[2048,2,128]{0,2,1:T(8,128)}, u32[]{:S(2)}) copy-start(f32[2048,2,128]{0,2,1:T(8,128)} %get-tuple-element.537) | copy-start | bytes 6291460 | tf_op jit(solution)/shard_map/while
  71.0 1.3 copy-start.5
  72.3 8.8 %copy-start.1 = (f32[1024,2,2,128]{0,3,2,1:T(8,128)S(1)}, f32[1024,2,2,128]{0,3,2,1:T(8,128)}, u32[]{:S(2)}) copy-start(f32[1024,2,2,128]{0,3,2,1:T(8,128)} %get-tuple-element.536) | copy-start | bytes 6291460 | tf_op jit(solution)/shard_map/while
  99.0 1.3 copy-start.2
  112.8 7.6 %copy-start.4 = (f32[2048,2,128]{0,2,1:T(8,128)S(1)}, f32[2048,2,128]{0,2,1:T(8,128)}, u32[]{:S(2)}) copy-start(f32[2048,2,128]{0,2,1:T(8,128)} %get-tuple-element.537) | copy-start | bytes 6291460 | tf_op jit(solution)/shard_map/while
  140.6 1.3 copy-start.5
  142.0 8.7 %copy-start.1 = (f32[1024,2,2,128]{0,3,2,1:T(8,128)S(1)}, f32[1024,2,2,128]{0,3,2,1:T(8,128)}, u32[]{:S(2)}) copy-start(f32[1024,2,2,128]{0,3,2,1:T(8,128)} %get-tuple-element.536) | copy-start | bytes 6291460 | tf_op jit(solution)/shard_map/while
  168.5 1.3 copy-start.2
  171.1 8.1 %collective-permute-start.2 = (bf16[1024,2,128]{0,2,1:T(8,128)(2,1)S(1)}, bf16[1024,2,128]{0,2,1:T(8,128)(2,1)S(1)}, u32[]{:S(2)}, u32[]{:S(2)}) collective-permute-start(bf16[1024,2,128]{0,2,1:T(8,128)(2,1)S(1)} %slice.51), channel_id=1, source_target_pairs={{4,0},{8,4},{12,8},{16,12},{20,16},{24,20},{28,24},{5,1},{9,5},{13... | collective-permute-start | bytes 1572872 | tf_op jit(solution)/shard_map/ppermute | solution.py:23
  173.7 6.0 %collective-permute-start.3 = (bf16[1024,2,128]{0,2,1:T(8,128)(2,1)S(1)}, bf16[1024,2,128]{0,2,1:T(8,128)(2,1)S(1)}, u32[]{:S(2)}, u32[]{:S(2)}) collective-permute-start(bf16[1024,2,128]{0,2,1:T(8,128)(2,1)S(1)} %slice.50), channel_id=1, source_target_pairs={{4,0},{8,4},{12,8},{16,12},{20,16},{24,20},{28,24},{5,1},{9,5},{13... | collective-permute-start | bytes 1572872 | tf_op jit(solution)/shard_map/ppermute | solution.py:23
  176.9 1.6 copy-start.3
  176.9 1.7 copy-start.9
  177.2 2.2 copy-start.6
  177.2 2.2 copy-start.8
  178.6 1.8 copy-start.7
  393.5 6.8 %copy-start = (bf16[5376,1024]{1,0:T(8,128)(2,1)S(1)}, bf16[5376,1024]{1,0:T(8,128)(2,1)}, u32[]{:S(2)}) copy-start(bf16[5376,1024]{1,0:T(8,128)(2,1)} %copy.36) | copy-start | bytes 33030148 | tf_op jit(solution)/shard_map/cond
Sparse Core Ops, SparseCore 0:
  9.6 195.1 all-gather.1
  224.3 153.2 all-reduce.2
where the time goes:
time: 413 us; the launch traced here: 412 us
  waiting for transfers between devices  176 us (43%)
  matrix products  163 us (39%)
  local copies, waits for them, and re-layouts  35.5 us (9%)
  between operations  14.9 us (4%)
  other arithmetic  12.1 us (3%)
  starting transfers between devices  9.57 us (2%)
    psum x1, waiting for transfers between devices, per_device(): gradient = lax.psum(partial_sum.astype(jnp.bfloat16), 'seq')  151 us
    dot_general x2, matrix products, one_block(): jnp.einsum('grqk,qgrh->kgh', grad_score, query_part, preferred_element_ty...  40.4 us
    dot_general x2, matrix products, one_block(): jnp.einsum('grqk,kgh->qgrh', grad_score, key_part, preferred_element_type...  35.6 us
    all_gather x1, waiting for transfers between devices, per_device(): lax.all_gather(inputs, 'head', axis=0, tiled=True)  23.9 us
    sub x2, matrix products, one_block(): exponent = jnp.where(allowed, jnp.exp(masked - row_top), 0.0)  23.5 us
    dot_general x1, matrix products, per_device(): lax.dot_general(lax.all_gather(inputs, 'head', axis=0, tiled=True), colum...  19.3 us
    another operation x3, local copies, waits for them, and re-layouts  17.8 us
    dot_general x2, matrix products, one_block(): jnp.einsum('grqk,qgrh->kgh', attend_low, out_part, preferred_element_type...  17.5 us
  transfers between devices with their start and end apart: 6, of which 2 were waited for; matrix products, arithmetic and copies ran while one was open for 38% of the time, Pallas kernels for 0%

commit v1 on v0

v1 whole, which is shorter than its diff:
```python
import functools

import jax
import jax.numpy as jnp
from jax import lax
from jax.experimental import pallas as pl
from jax.experimental.pallas import tpu as pltpu
from jax.sharding import PartitionSpec as P

D = 5376
HD = 128
KV_DEV = 2
QPK = 2
WINDOW = 1024
BLOCK = 1024
NBLK = 6


score_scale = 168.0 ** (-0.5)
log2_e = 1.4426950408889634
rotary_frequency_base = 10000.0
neg_large = -1e30


CHUNK = 128
CHUNKS = BLOCK // CHUNK
MESH = pl.DeviceIdType.MESH


def rope_tables(positions, head_size):
    half_size = head_size // 2
    frequency = jnp.power(
        rotary_frequency_base, -2.0 * jnp.arange(half_size, dtype=jnp.float32) / head_size
    )
    angles = frequency[:, None] * positions.astype(jnp.float32)[None, :]
    return (jnp.cos(angles), jnp.sin(angles))


def unrotate(gradient, cosine, sine):
    first, second = gradient[: HD // 2], gradient[HD // 2 :]
    return jnp.concatenate([first * cosine + second * sine, second * cosine - first * sine], 0)


def dot(left, right, left_dim, right_dim):
    return lax.dot_general(
        left, right, (((left_dim,), (right_dim,)), ((), ())), preferred_element_type=jnp.float32
    )


def layer_kernel(
    sizes,
    pick_ref,
    band_ref,
    cos_ref,
    sin_ref,
    inputs_ref,
    query_ref,
    out_ref,
    key_ref,
    value_ref,
    block_ref,
    layer,
    grads,
    keys,
    vals,
    rim_out,
    rim_in,
    totals,
    pieces,
    pair_out,
    pair_in,
    kept,
    chip_out,
    chip_in,
    kv_send,
    kv_recv,
    rim_send,
    rim_recv,
    up_send,
    up_recv,
    down_send,
    down_recv,
    pair_send,
    pair_recv,
    chip_send,
    chip_recv,
):
    tok_rows, seq_count, head_count = sizes
    part_rows = tok_rows // head_count
    chips = seq_count // 2
    hops = head_count - 1
    block_rows = min(256, tok_rows)
    span_rows = block_rows + WINDOW
    seq = lax.axis_index("seq")
    group = lax.axis_index("head")
    core = lax.rem(seq, 2)
    chip = lax.div(seq, 2)
    sibling = seq + 1 - 2 * core
    beside = seq - 1 + 2 * core
    has_beside = (beside >= 0) & (beside < seq_count)
    has_above = group + 1 < head_count
    has_below = group >= 1
    has_next = seq + 1 < seq_count
    has_previous = seq >= 1

    barrier = pltpu.get_barrier_semaphore()

    def greet(seq_at, group_at):
        pl.semaphore_signal(barrier, inc=1, device_id=(seq_at, group_at), device_id_type=MESH)

    def other_chip(d):
        return 2 * lax.rem(chip + d, chips) + core

    greet(sibling, group)
    for d in range(1, chips):
        greet(other_chip(d), group)
    for condition, seq_at, group_at in (
        (has_beside, beside, group),
        (has_above, seq, group + 1),
        (has_below, seq, group - 1),
    ):
        pl.when(condition)(functools.partial(greet, seq_at, group_at))
    peers = chips + sum(
        jnp.where(condition, 1, 0) for condition in (has_beside, has_above, has_below)
    )
    pl.semaphore_wait(barrier, peers)

    def remote(source, target, send, recv, seq_at, group_at):
        return pltpu.make_async_remote_copy(
            src_ref=source,
            dst_ref=target,
            send_sem=send,
            recv_sem=recv,
            device_id=(seq_at, group_at),
            device_id_type=MESH,
        )

    def kv_copy(i, source, joined):
        target = joined.at[pl.ds(0, tok_rows)]
        return remote(source, target, kv_send.at[i], kv_recv.at[i], seq + 1, group)

    @pl.when(has_next)
    def _():
        kv_copy(0, key_ref, keys).start()
        kv_copy(1, value_ref, vals).start()

    widths = [
        CHUNK * sum(b * BLOCK + c * CHUNK < D for b in range(NBLK)) for c in range(CHUNKS)
    ]

    def shard_rows(shard):
        return pl.ds(pl.multiple_of(shard * part_rows, part_rows), part_rows)

    def layer_part(c, shard):
        return layer.at[c, shard_rows(shard), pl.ds(0, widths[c])]

    def up_copy(k, c, shard):
        part = layer_part(c, shard)
        return remote(part, part, up_send.at[k, c], up_recv.at[k, c], seq, group + 1)

    def down_copy(k, c, shard):
        part = layer_part(c, shard)
        return remote(part, part, down_send.at[k, c], down_recv.at[k, c], seq, group - 1)

    def arrive(k, c):
        @pl.when(group - 1 - k >= 0)
        def _():
            up_copy(k, c, group - 1 - k).wait_recv()

        @pl.when(group + 1 + k < head_count)
        def _():
            down_copy(k, c, group + 1 + k).wait_recv()

    def sends(k):
        return (
            ((group - k >= 0) & has_above, up_copy, group - k),
            ((group + k < head_count) & has_below, down_copy, group + k),
        )

    def issue(k, c):
        if k > 0:
            arrive(k - 1, c)
        for condition, make, shard in sends(k):

            @pl.when(condition)
            def _(make=make, shard=shard):
                make(k, c, shard).start()

    def ahead(k):
        return min(CHUNKS, 2 * (hops - k))

    for c in range(CHUNKS):
        for b in range(widths[c] // CHUNK):
            low = b * BLOCK + c * CHUNK
            layer[c, shard_rows(group), b * CHUNK : (b + 1) * CHUNK] = inputs_ref[
                :, low : low + CHUNK
            ]
        if c < ahead(0):
            issue(0, c)

    keys[tok_rows:] = key_ref[...]
    vals[tok_rows:] = value_ref[...]

    @pl.when(has_previous)
    def _():
        kv_copy(0, key_ref, keys).wait_recv()
        kv_copy(1, value_ref, vals).wait_recv()

    @pl.when(jnp.logical_not(has_previous))
    def _():
        keys[:tok_rows] = jnp.zeros((tok_rows, KV_DEV * HD), jnp.bfloat16)
        vals[:tok_rows] = jnp.zeros((tok_rows, KV_DEV * HD), jnp.bfloat16)

    def rim_copy(g):
        return remote(
            rim_out.at[g], rim_in.at[g], rim_send.at[g], rim_recv.at[g], seq - 1, group
        )

    own = lax.broadcasted_iota(jnp.int32, (1, block_rows), 1) + WINDOW
    own = jnp.concatenate([own] * QPK, 1)

    for g in range(KV_DEV):
        lanes = slice(g * HD, (g + 1) * HD)
        totals[g] = jnp.zeros((2, 2 * tok_rows, HD), jnp.float32)

        @pl.loop(0, tok_rows // block_rows)
        def _(step, g=g, lanes=lanes):
            offset = pl.multiple_of(step * block_rows, block_rows)
            rows = pl.ds(offset, block_rows)
            span = pl.ds(pl.multiple_of(tok_rows - WINDOW + offset, 128), span_rows)
            key_part = keys[span, lanes]
            value_part = vals[span, lanes]
            heads = [slice(q * HD, (q + 1) * HD) for q in range(g * QPK, (g + 1) * QPK)]
            query_part = jnp.concatenate([query_ref[rows, head] for head in heads], 0)
            out_part = jnp.concatenate([out_ref[rows, head] for head in heads], 0)
            band = band_ref[:, rows] - (offset - WINDOW)
            band = jnp.concatenate([band] * QPK, 1)
            key_at = lax.broadcasted_iota(jnp.int32, (span_rows, QPK * block_rows), 0)

            scores = dot(key_part, query_part, 1, 1)
            scores = jnp.where((key_at >= band) & (key_at <= own), scores, neg_large)
            row_top = jnp.max(scores, 0, keepdims=True)
            exponent = jnp.exp2((scores - row_top) * (score_scale * log2_e))
            inverse = 1.0 / jnp.sum(exponent, 0, keepdims=True)
            grad_attend = dot(value_part, out_part, 1, 1)
            attend = exponent * inverse
            row_dot = jnp.sum(attend * grad_attend, 0, keepdims=True)
            attend_low = attend.astype(jnp.bfloat16)
            grad_score = (attend * (grad_attend - row_dot) * score_scale).astype(jnp.bfloat16)
            totals[g, 0, span, :] += dot(grad_score, query_part, 1, 0)
            totals[g, 1, span, :] += dot(attend_low, out_part, 1, 0)
            grad_query = dot(key_part, grad_score, 0, 0)
            cosine = cos_ref[:, rows]
            sine = sin_ref[:, rows]
            for r, head in enumerate(heads):
                part = grad_query[:, r * block_rows : (r + 1) * block_rows]
                grads[head, rows] = unrotate(part, cosine, sine).astype(jnp.bfloat16)

        rim_out[g] = totals[g, :, :tok_rows].astype(jnp.bfloat16)

        @pl.when(has_previous)
        def _(g=g):
            rim_copy(g).start()

        if g < KV_DEV - 1:
            for k in range(1, min(2, hops)):
                for c in range(2):
                    issue(k, c)

    for k in range(1, hops):
        for c in range(2 if k == 1 else 0, ahead(k)):
            issue(k, c)

    for g in range(KV_DEV):

        @pl.when(has_next)
        def _(g=g):
            rim_copy(g).wait_recv()

        @pl.when(jnp.logical_not(has_next))
        def _(g=g):
            rim_in[g] = jnp.zeros((2, tok_rows, HD), jnp.bfloat16)

        grad_key = totals[g, 0, tok_rows:] + rim_in[g, 0].astype(jnp.float32)
        grad_value = totals[g, 1, tok_rows:] + rim_in[g, 1].astype(jnp.float32)
        first = (KV_DEV * QPK + g) * HD
        grads[first : first + HD, :] = unrotate(grad_key.T, cos_ref[...], sin_ref[...]).astype(
            jnp.bfloat16
        )
        first += KV_DEV * HD
        grads[first : first + HD, :] = grad_value.T.astype(jnp.bfloat16)

    pieces[...] = jnp.zeros(pieces.shape, jnp.bfloat16)

    def pair_copy(slot):
        return remote(
            pair_out.at[slot], pair_in.at[slot], pair_send.at[slot], pair_recv.at[slot], sibling, group
        )

    def chip_copy(slot, d):
        return remote(
            chip_out.at[slot, d - 1],
            chip_in.at[slot, d - 1],
            chip_send.at[slot, d - 1],
            chip_recv.at[slot, d - 1],
            other_chip(d),
            group,
        )

    def finish(c):
        slot = c % 2
        total = kept[slot].astype(jnp.float32)
        for d in range(1, chips):
            chip_copy(slot, d).wait()
            total += chip_in[slot, d - 1].astype(jnp.float32)
        block_ref[:, c * CHUNK : (c + 1) * CHUNK] = total.astype(jnp.bfloat16)

    for c in range(CHUNKS):
        slot = c % 2
        for k in range(hops - 1, -1, -1):
            if ahead(k) <= c + 2 * (hops - k) < CHUNKS:
                issue(k, c + 2 * (hops - k))
        arrive(hops - 1, c)
        if c > 0 and widths[c] < widths[c - 1]:
            for b in range(widths[c] // CHUNK, widths[c - 1] // CHUNK):
                pieces[b] = jnp.zeros((pieces.shape[1], CHUNK), jnp.bfloat16)
        product = dot(grads[...], layer[c, :, : widths[c]], 1, 0).astype(jnp.bfloat16)
        for b in range(widths[c] // CHUNK):
            pieces[b] = product[:, b * CHUNK : (b + 1) * CHUNK]
        for j in range(chips):
            pair_out[slot, j] = pieces[pick_ref[2 * j + 1 - core]]
        pair_copy(slot).start()
        pair_copy(slot).wait()
        if c > 0:
            finish(c - 1)
        kept[slot] = (
            pieces[pick_ref[2 * chip + core]].astype(jnp.float32)
            + pair_in[slot, chip].astype(jnp.float32)
        ).astype(jnp.bfloat16)
        for d in range(1, chips):
            at = lax.rem(chip + d, chips)
            chip_out[slot, d - 1] = (
                pieces[pick_ref[2 * at + core]].astype(jnp.float32)
                + pair_in[slot, at].astype(jnp.float32)
            ).astype(jnp.bfloat16)
            chip_copy(slot, d).start()
    finish(CHUNKS - 1)

    @pl.when(has_next)
    def _():
        kv_copy(0, key_ref, keys).wait_send()
        kv_copy(1, value_ref, vals).wait_send()

    @pl.when(has_previous)
    def _():
        for g in range(KV_DEV):
            rim_copy(g).wait_send()

    for k in range(hops):
        for condition, make, shard in sends(k):

            @pl.when(condition)
            def _(make=make, shard=shard, k=k):
                for c in range(CHUNKS):
                    make(k, c, shard).wait_send()


def owned_block(pick, band, cosine, sine, inputs, queries, out_grad, key_rows, values):
    tok_rows = queries.shape[0]
    seq_count = lax.axis_size("seq")
    head_count = lax.axis_size("head")
    chips = seq_count // 2
    hops = head_count - 1
    columns = KV_DEV * (QPK + 2) * HD
    low = jnp.bfloat16
    dma = pltpu.SemaphoreType.DMA
    vmem = pl.BlockSpec(memory_space=pltpu.VMEM)
    return pl.pallas_call(
        functools.partial(layer_kernel, (tok_rows, seq_count, head_count)),
        in_specs=[pl.BlockSpec(memory_space=pltpu.SMEM)] + [vmem] * 8,
        out_specs=vmem,
        out_shape=jax.ShapeDtypeStruct((columns, BLOCK), low),
        scratch_shapes=[
            pltpu.VMEM((CHUNKS, tok_rows, NBLK * CHUNK), low),
            pltpu.VMEM((columns, tok_rows), low),
            pltpu.VMEM((2 * tok_rows, KV_DEV * HD), low),
            pltpu.VMEM((2 * tok_rows, KV_DEV * HD), low),
            pltpu.VMEM((KV_DEV, 2, tok_rows, HD), low),
            pltpu.VMEM((KV_DEV, 2, tok_rows, HD), low),
            pltpu.VMEM((KV_DEV, 2, 2 * tok_rows, HD), jnp.float32),
            pltpu.VMEM((NBLK + 1, columns, CHUNK), low),
            pltpu.VMEM((2, chips, columns, CHUNK), low),
            pltpu.VMEM((2, chips, columns, CHUNK), low),
            pltpu.VMEM((2, columns, CHUNK), low),
            pltpu.VMEM((2, chips - 1, columns, CHUNK), low),
            pltpu.VMEM((2, chips - 1, columns, CHUNK), low),
            dma((2,)),
            dma((2,)),
            dma((KV_DEV,)),
            dma((KV_DEV,)),
            dma((hops, CHUNKS)),
            dma((hops, CHUNKS)),
            dma((hops, CHUNKS)),
            dma((hops, CHUNKS)),
            dma((2,)),
            dma((2,)),
            dma((2, chips - 1)),
            dma((2, chips - 1)),
        ],
        compiler_params=pltpu.CompilerParams(
            collective_id=0, has_side_effects=True, vmem_limit_bytes=60 * 2**20
        ),
        name="owned_block",
    )(pick, band, cosine, sine, inputs, queries, out_grad, key_rows, values)


def per_device(inputs, queries, key_rows, values, out_grad, band_start, owners):
    tok_rows = queries.shape[0]
    seq_count = lax.axis_size("seq")
    seq_index = lax.axis_index("seq")
    group_index = lax.axis_index("head")
    tokens_all = tok_rows * seq_count
    positions = seq_index * tok_rows + jnp.arange(tok_rows, dtype=jnp.int32)
    cosine, sine = rope_tables(positions, HD)
    owner_row = lax.dynamic_index_in_dim(owners, group_index, 0, keepdims=False)
    held = owner_row[None, :] == jnp.arange(seq_count, dtype=jnp.int32)[:, None]
    order = jnp.arange(NBLK, dtype=jnp.int32)[None, :]
    pick = NBLK + jnp.sum(jnp.where(held, order - NBLK, 0), 1, dtype=jnp.int32)
    band = (band_start - seq_index * tok_rows)[None, :]
    block = owned_block(
        pick, band, cosine, sine, inputs, queries, out_grad, key_rows, values
    )
    left_stat = dot(block, block, 0, 0) / tokens_all
    right_stat = dot(block, block, 1, 1) / tokens_all
    return (left_stat[None, None], right_stat[None, None])


def solution(mesh):
    in_specs = (
        P(("seq", "head"), None),
        P("seq", "head"),
        P("seq", "head"),
        P("seq", "head"),
        P("seq", "head"),
        P("seq"),
        P(),
    )
    out_specs = (P("seq", "head", None, None), P("seq", "head", None, None))
    return jax.shard_map(
        per_device, mesh=mesh, in_specs=in_specs, out_specs=out_specs, check_vma=False
    )
```

time: 413 us -> 237 us (0.57)
  Pallas kernels: 0 us -> 221 us
  waiting for transfers between devices: 176 us -> 0 us
  matrix products: 163 us -> 11.2 us
  local copies, waits for them, and re-layouts: 35.5 us -> 0.68 us
  between operations: 14.9 us -> 0.66 us
  starting transfers between devices: 9.57 us -> 0 us
  other arithmetic: 12.1 us -> 3.69 us
    pallas_call x0 -> x1, Pallas kernels: none -> 221 us  [owned_block(): pl.pallas_call(functools.partial(layer_kernel, (tok_rows, seq_count, head...]
    psum x1 -> x0, waiting for transfers between devices: 151 us -> none  [per_device(): gradient = lax.psum(partial_sum.astype(jnp.bfloat16), 'seq')]
    dot_general x11 -> x2, matrix products: 139 us -> 11.2 us  [dot(): lax.dot_general(left, right, (((left_dim,), (right_dim,)), ((), ())), pre...]
    all_gather x1 -> x0, waiting for transfers between devices: 23.9 us -> none  [per_device(): lax.all_gather(inputs, 'head', axis=0, tiled=True)]
    sub x2 -> x0, matrix products: 23.5 us -> none  [one_block(): exponent = jnp.where(allowed, jnp.exp(masked - row_top), 0.0)]
    another operation x3 -> x0, local copies, waits for them, and re-layouts: 17.8 us -> none
    ppermute x4 -> x0, starting transfers between devices: 9.49 us -> none  [shifted(): lax.ppermute(value, axis, [(source, source + steps) for source in range(i...]
    unnamed x18 -> x4, local copies, waits for them, and re-layouts: 8.15 us -> 0.68 us
  transfers between devices with their start and end apart: 6 -> 0, of which waited for: 2 -> 0; matrix products, arithmetic and copies ran while one was open for 38% -> 0% of each run, Pallas kernels for 0% -> 0%
where the time goes in v1:
time: 237 us
  Pallas kernels  221 us (93%)
  matrix products  11.2 us (5%)
  other arithmetic  3.69 us (2%)
    pallas_call x1, Pallas kernels, owned_block(): pl.pallas_call(functools.partial(layer_kernel, (tok_rows, seq_count, head...  221 us
    dot_general x2, matrix products, dot(): lax.dot_general(left, right, (((left_dim,), (right_dim,)), ((), ())), pre...  11.2 us

profile of v1, /device:TPU:0, one launch (start us, length us, event | category | flops | bytes accessed | tf_op | source)
XLA Modules:
  0.0 237.2 jit_solution(7001241597939140583)
XLA Ops:
  0.6 0.0 copy-start
  0.7 0.7 copy-done
  1.3 0.1 select_reduce_fusion
  1.4 0.5 broadcast_add_fusion.pick_ref
  1.9 1.3 add_convert_fusion
  3.2 1.8 multiply_sine_fusion
  5.0 221.0 %owned_block.1 = bf16[1024,1024]{1,0:T(8,128)(2,1)} custom-call(s32[8]{0:T(128)} %broadcast_add_fusion.pick_ref, s32[1,1024]{1,0:T(1,128)} %bitcast.11, f32[64,1024]{1,0:T(8,128)} %get-tuple-element.3.cos_ref, f32[64,1024]{1,0:T(8,128)} %get-tuple-element.2.sin_ref, bf16[256,5376]{1,0:T(8,128)(2,1)} %inputs_ref.1, bf16[1024,512]{1,0:T(8,128)(2,1)} %query_ref.1, ...), custom_call_target="tpu_custom_call" | custom-call | tf_op jit(solution)/shard_map/owned_block/pallas_call | solution.py:378
  226.0 0.0 copy-start.1
  226.0 6.8 %multiply_bitcast_fusion = f32[1,1,1024,1024]{3,2,1,0:T(8,128)} fusion(bf16[1024,1024]{1,0:T(8,128)(2,1)} %owned_block.1), kind=kOutput, calls=%fused_computation | convolution fusion | flops 2148532224 | bytes 6291456 | tf_op jit(solution)/shard_map/dot_general | solution.py:45
  232.8 0.0 copy-done.1
  232.8 4.4 %multiply_bitcast_fusion.1 = f32[1,1,1024,1024]{3,2,1,0:T(8,128)} fusion(bf16[1024,1024]{1,0:T(8,128)(2,1)S(1)} %copy-done.1), kind=kOutput, calls=%fused_computation.1 | convolution fusion | flops 2148532224 | bytes 6291456 | tf_op jit(solution)/shard_map/dot_general | solution.py:45
  (3 shorter events, 0.0 us)
Async XLA Ops:
  0.6 0.7 copy-start
  226.0 6.8 %copy-start.1 = (bf16[1024,1024]{1,0:T(8,128)(2,1)S(1)}, bf16[1024,1024]{1,0:T(8,128)(2,1)}, u32[]{:S(2)}) copy-start(bf16[1024,1024]{1,0:T(8,128)(2,1)} %owned_block.1) | copy-start | bytes 6291460
